TPU v7x, 256 devices: a whole 4x4x8 slice. The times are simulated.
256 devices in a mesh: blk: 128 (over y, z_lo, x, core), head: 2 (over z_hi).
Axes of the slice: x: 4, y: 4, z: 8 (z_hi: 2, z_lo: 4; z = z_hi * 4 + z_lo), core: 2. Of those that a mesh axis runs over, the one named last changes fastest.
Arguments:
- queries: bfloat16 [65536, 3584], P(('blk', 'head')), may hold values from -5 to 5
- keys: bfloat16 [65536, 512], P(('blk', 'head')), may hold values from -5 to 5
- values: bfloat16 [65536, 512], P(('blk', 'head')), may hold values from -6 to 6
- kept: int32 [512, 8], P('blk'), may hold values from 0 to 511, as said below
- frame_ids: int32 [65536], replicated, may hold values from 0 to 256, as said below
Outputs:
- attended: bfloat16 [65536, 3584], P(('blk', 'head'))
Inputs may be any that keep to these rules, and one draw needn't show every extreme that they name: Row t of kept lists key tiles k with t - 12 < k <= t; its first entry is t; entries may repeat. `frame_ids`: never falls along the sequence; frames begin only at even positions; the first token is in frame 0 and the last frame is 256.
All inputs are finite; a program needn't handle non-finite values.
Results may differ from a plain program's by a relative error of at most 0.008.
Values may be sent and summed in bfloat16 or wider, within the bound.
No kernel may reach another device: no remote copies, remote signals or barrier semaphores. Data moves between devices by JAX's collectives and lax.ppermute only.
A program may use at most 192 MiB of HBM per device.

v0:
```python
import math

import jax
import jax.numpy as jnp
from jax import lax
from jax.experimental import pallas as pl
from jax.experimental.pallas import tpu as pltpu
from jax.sharding import PartitionSpec as P

QUERY_HEADS = 28
KEY_VALUE_HEADS = 4
GROUP = QUERY_HEADS // KEY_VALUE_HEADS
HEAD_SIZE = 128
TILE = 128
TOKENS = 256
KEPT = 8
BLOCKS = 10
TURN = 16
AXES = ("blk", "head")
HEAD_GROUPS = ((0, 2), (2, 2))
SCALE = math.log2(math.e) / math.sqrt(HEAD_SIZE)
NEVER = -1e30


def device(chip, core, half):
    return (chip * 2 + core) * 2 + half


def across_halves(chips):
    return [
        (device(c, k, h), device(c, k, 1 - h)) for c in range(chips) for k in (0, 1) for h in (0, 1)
    ]


def turns(chip):
    return chip % TURN == 0


def next_chip(chips):
    pairs = []
    for c in range(chips):
        after = (c + 1) % chips
        for k in (0, 1):
            for h in (0, 1):
                pairs.append((device(c, k, h), device(after, k, 1 - h if turns(after) else h)))
    return pairs


def other_core(chips):
    return [
        (device(c, k, h), device(c, 1 - k, h)) for c in range(chips) for k in (0, 1) for h in (0, 1)
    ]


def second_next_chip(chips, halves):
    return [
        (device(c, 1, h), device((c + 2) % chips, 0, h)) for c in range(chips) for h in halves
    ]


def attend_kernel(heads, first_head, *refs):
    where, bias, q, tail, cross_tail = refs[:5]
    blocks = refs[5:13]
    out, keys, values, kept_keys, kept_values = refs[-5:]

    def place(head, slot, block):
        rows = pl.ds(pl.multiple_of(slot * TOKENS, TOKENS), TOKENS)
        keys[head, rows, :] = block[:, :HEAD_SIZE]
        values[head, rows, :] = block[:, HEAD_SIZE:]

    for head in range(heads):
        place(head, 1, cross_tail[:, pl.ds(head * 2 * HEAD_SIZE, 2 * HEAD_SIZE)])
        rows = pl.ds(pl.multiple_of(where[2, 8], TILE), TILE)
        last = tail[:, pl.ds(head * 2 * HEAD_SIZE, 2 * HEAD_SIZE)]
        keys[head, rows, :] = last[:, :HEAD_SIZE]
        values[head, rows, :] = last[:, HEAD_SIZE:]
        for number, block in enumerate(blocks):
            place(head, where[2, number], block[:, pl.ds(head * 2 * HEAD_SIZE, 2 * HEAD_SIZE)])
        for tile in range(2):
            for entry in range(KEPT):
                index = where[tile, entry]
                rows = pl.ds(pl.multiple_of(index * TILE, TILE), TILE)
                slot = pl.ds(entry * TILE, TILE)
                key = keys[head, rows, :]
                value = values[head, rows, :]
                count = jnp.float32(1.0)
                if entry:
                    again = index == where[tile, 0]
                    key = jnp.where(again, jnp.broadcast_to(key[0:1, :], key.shape), key)
                    for earlier in range(1, entry):
                        again = again | (index == where[tile, earlier])
                    value = jnp.where(again, jnp.zeros_like(value), value)
                    count = jnp.where(again, 0.0, 1.0)
                kept_keys[head, tile, slot, :] = key
                kept_values[head, tile, slot, :HEAD_SIZE] = value
                kept_values[head, tile, slot, HEAD_SIZE:] = jnp.full(
                    value.shape, count.astype(jnp.bfloat16)
                )
        for tile in range(2):
            for member in range(GROUP):
                rows = pl.ds(tile * TILE, TILE)
                columns = pl.ds((head * GROUP + member) * HEAD_SIZE, HEAD_SIZE)
                scores = lax.dot_general(
                    q[rows, columns],
                    kept_keys[head, tile],
                    (((1,), (1,)), ((), ())),
                    preferred_element_type=jnp.float32,
                )
                scores = jnp.concatenate(
                    [scores[:, :TILE] + bias[tile], scores[:, TILE:]], axis=1
                )
                top = jnp.max(scores, axis=1, keepdims=True)
                weights = jnp.exp2((scores - top) * SCALE).astype(jnp.bfloat16)
                summed = jnp.dot(weights, kept_values[head, tile], preferred_element_type=jnp.float32)
                result = summed[:, :HEAD_SIZE] / summed[:, HEAD_SIZE:]
                out[rows, columns] = result.astype(jnp.bfloat16)


def pack_kernel(keys, values, own, tail, *parts):
    for head in range(KEY_VALUE_HEADS):
        columns = pl.ds(head * HEAD_SIZE, HEAD_SIZE)
        own[:, pl.ds(head * 2 * HEAD_SIZE, HEAD_SIZE)] = keys[:, columns]
        own[:, pl.ds((head * 2 + 1) * HEAD_SIZE, HEAD_SIZE)] = values[:, columns]
        tail[:, pl.ds(head * 2 * HEAD_SIZE, HEAD_SIZE)] = keys[TILE:, columns]
        tail[:, pl.ds((head * 2 + 1) * HEAD_SIZE, HEAD_SIZE)] = values[TILE:, columns]
    for (first, count), part in zip(HEAD_GROUPS, parts):
        for head in range(count):
            columns = pl.ds((first + head) * HEAD_SIZE, HEAD_SIZE)
            part[:, pl.ds(head * 2 * HEAD_SIZE, HEAD_SIZE)] = keys[:, columns]
            part[:, pl.ds((head * 2 + 1) * HEAD_SIZE, HEAD_SIZE)] = values[:, columns]


def pack(keys, values):
    whole = pl.BlockSpec(memory_space=pltpu.VMEM)
    widths = [count * 2 * HEAD_SIZE for _, count in HEAD_GROUPS]
    shapes = [(TOKENS, 2 * KEY_VALUE_HEADS * HEAD_SIZE), (TILE, 2 * KEY_VALUE_HEADS * HEAD_SIZE)]
    shapes += [(TOKENS, width) for width in widths]
    return pl.pallas_call(
        pack_kernel,
        out_shape=[jax.ShapeDtypeStruct(shape, jnp.bfloat16) for shape in shapes],
        in_specs=[whole, whole],
        out_specs=[whole] * len(shapes),
        name="pack",
    )(keys, values)


def attend(group, where, bias, queries, shared, own_group, previous):
    first_head, heads = group
    width = heads * GROUP * HEAD_SIZE
    part = heads * 2 * HEAD_SIZE
    number = first_head // heads
    whole = pl.BlockSpec(memory_space=pltpu.VMEM)
    tail, *shared = shared
    cross_tail, *own_group = own_group
    operands = [where, bias, queries, tail, cross_tail, *shared, *own_group]
    specs = [
        pl.BlockSpec(memory_space=pltpu.SMEM),
        whole,
        pl.BlockSpec((TOKENS, width), lambda i: (0, number)),
        pl.BlockSpec((TILE, part), lambda i: (0, number)),
        whole,
    ]
    specs += [pl.BlockSpec((TOKENS, part), lambda i: (0, number))] * len(shared)
    specs += [whole] * len(own_group)
    aliases = {}
    if previous is not None:
        aliases = {len(operands): 0}
        operands.append(previous)
        specs.append(pl.BlockSpec(memory_space=pl.ANY))
    scores = heads * GROUP * 2 * TILE * KEPT * TILE
    return pl.pallas_call(
        lambda *refs: attend_kernel(heads, first_head, *refs),
        grid=(1,),
        out_shape=jax.ShapeDtypeStruct(queries.shape, jnp.bfloat16),
        in_specs=specs,
        out_specs=pl.BlockSpec((TOKENS, width), lambda i: (0, number)),
        scratch_shapes=[
            pltpu.VMEM((heads, BLOCKS * TOKENS, HEAD_SIZE), jnp.bfloat16),
            pltpu.VMEM((heads, BLOCKS * TOKENS, HEAD_SIZE), jnp.bfloat16),
            pltpu.VMEM((heads, 2, KEPT * TILE, HEAD_SIZE), jnp.bfloat16),
            pltpu.VMEM((heads, 2, KEPT * TILE, 2 * HEAD_SIZE), jnp.bfloat16),
        ],
        input_output_aliases=aliases,
        compiler_params=pltpu.CompilerParams(vmem_limit_bytes=32 * 2**20),
        cost_estimate=pl.CostEstimate(
            flops=4 * scores * HEAD_SIZE, bytes_accessed=2 * 2**20, transcendentals=scores
        ),
        name="attend",
    )(*operands)


def shards(queries, keys, values, kept, frame_ids):
    chips = lax.axis_size("blk") // 2
    blk = lax.axis_index("blk")
    half = lax.axis_index("head")
    core = blk % 2

    def move(value, pairs):
        return lax.ppermute(value, AXES, pairs)

    own, last, *parts = pack(keys, values)
    crosses = [move(parts[0], across_halves(chips))]
    before = move(own, next_chip(chips))
    core_own = move(own, other_core(chips))
    tail = move(last, second_next_chip(chips, (0, 1)))
    tokens = lax.dynamic_slice_in_dim(frame_ids, (blk * 2 + half) * TOKENS, TOKENS, 0)
    frames = tokens.reshape(2, TILE)
    bias = jnp.where(frames[:, None, :] <= frames[:, :, None], 0.0, NEVER).astype(jnp.float32)
    rows = lax.dynamic_slice_in_dim(kept, half * 2, 2, 0) - (blk // 2) * 8 + 12
    other = 1 - core
    far = 1 - half
    near = jnp.where(turns(blk // 2), far, half)
    slots = jnp.stack(
        [
            6 + 2 * core + half,
            2 + 2 * core + near,
            6 + 2 * other + half,
            2 + 2 * other + near,
            6 + 2 * core + far,
            2 + 2 * core + 1 - near,
            6 + 2 * other + far,
            2 + 2 * other + 1 - near,
            (2 * half + 1) * TILE,
        ]
    )
    where = jnp.zeros((3, 16), jnp.int32)
    where = lax.dynamic_update_slice(where, rows, (0, 0))
    where = lax.dynamic_update_slice(where, slots[None, :].astype(jnp.int32), (2, 0))

    before, core_own, tail = lax.optimization_barrier((before, core_own, tail))
    core_before = move(before, other_core(chips))
    result = None
    waited = (before, core_own, tail)
    for number, group in enumerate(HEAD_GROUPS):
        cross = crosses[number]
        if number + 1 < len(HEAD_GROUPS):
            sent, waited = lax.optimization_barrier((parts[number + 1], waited))
            crosses.append(move(sent, across_halves(chips)))
        cross_before = move(cross, next_chip(chips))
        core_cross = move(cross, other_core(chips))
        cross_tail = move(cross, second_next_chip(chips, (0,)))
        if number + 1 < len(HEAD_GROUPS):
            (cross_before, core_cross, cross_tail, core_before, crosses[-1]) = (
                lax.optimization_barrier(
                    (cross_before, core_cross, cross_tail, core_before, crosses[-1])
                )
            )
        core_cross_before = move(cross_before, other_core(chips))
        shared = (tail, own, before, core_own, core_before)
        own_group = (cross_tail, cross, cross_before, core_cross, core_cross_before)
        result = attend(group, where, bias, queries, shared, own_group, result)
    return result


def solution(mesh):
    placed = (
        P(AXES, None),
        P(AXES, None),
        P(AXES, None),
        P("blk", None),
        P(),
    )
    return jax.shard_map(
        shards, mesh=mesh, in_specs=placed, out_specs=P(AXES, None), check_vma=False
    )
```

profile of v0, /device:TPU:121, one launch (start us, length us, event | category | flops | bytes accessed | tf_op | source)
XLA Modules:
  0.0 89.9 jit_solution(14315673078908278006)
XLA Ops:
  0.0 2.4 %pack.1 = (bf16[256,1024]{1,0:T(8,128)(2,1)}, bf16[128,1024]{1,0:T(8,128)(2,1)}, bf16[256,512]{1,0:T(8,128)(2,1)}, bf16[256,512]{1,0:T(8,128)(2,1)}) custom-call(bf16[256,512]{1,0:T(8,128)(2,1)} %keys.1, bf16[256,512]{1,0:T(8,128)(2,1)} %values.1), custom_call_target="tpu_custom_call" | custom-call | tf_op jit(solution)/shard_map/pack/pallas_call | solution.py:138
  2.4 0.7 collective-permute-start.1
  3.1 1.2 %collective-permute-start = (bf16[256,1024]{1,0:T(8,128)(2,1)}, bf16[256,1024]{1,0:T(8,128)(2,1)S(1)}, u32[]{:S(2)}, u32[]{:S(2)}) collective-permute-start(bf16[256,1024]{1,0:T(8,128)(2,1)} %get-tuple-element.18.refs_5_), channel_id=1, source_target_pairs={{0,4},{1,5},{2,6},{3,7},{4,8},{5,9},{6,10},{7,11},{8,12},{9,13},{1... | collective-permute-start | bytes 1572872 | tf_op jit(solution)/shard_map/ppermute | solution.py:199
  4.3 4.5 %collective-permute-start.2 = (bf16[128,1024]{1,0:T(8,128)(2,1)}, bf16[128,1024]{1,0:T(8,128)(2,1)S(1)}, u32[]{:S(2)}, u32[]{:S(2)}) collective-permute-start(bf16[128,1024]{1,0:T(8,128)(2,1)} %get-tuple-element.19), channel_id=1, source_target_pairs={{2,8},{3,9},{6,12},{7,13},{10,16},{11,17},{14,20},{15,21},{18,24},... | collective-permute-start | bytes 786440 | tf_op jit(solution)/shard_map/ppermute | solution.py:199
  8.8 4.3 %collective-permute-start.3 = (bf16[256,512]{1,0:T(8,128)(2,1)}, bf16[256,512]{1,0:T(8,128)(2,1)S(1)}, u32[]{:S(2)}, u32[]{:S(2)}) collective-permute-start(bf16[256,512]{1,0:T(8,128)(2,1)} %get-tuple-element.21), channel_id=1, source_target_pairs={{0,1},{1,0},{2,3},{3,2},{4,5},{5,4},{6,7},{7,6},{8,9},{9,8},{10,11... | collective-permute-start | bytes 786440 | tf_op jit(solution)/shard_map/ppermute | solution.py:199
  13.1 6.0 %collective-permute-done.2.refs_3_ = bf16[128,1024]{1,0:T(8,128)(2,1)S(1)} collective-permute-done((bf16[128,1024]{1,0:T(8,128)(2,1)}, bf16[128,1024]{1,0:T(8,128)(2,1)S(1)}, u32[]{:S(2)}, u32[]{:S(2)}) %collective-permute-start.2) | collective-permute-done | bytes 262176 | tf_op jit(solution)/shard_map/ppermute | solution.py:199
  19.2 2.7 %collective-permute-done.refs_6_ = bf16[256,1024]{1,0:T(8,128)(2,1)S(1)} collective-permute-done((bf16[256,1024]{1,0:T(8,128)(2,1)}, bf16[256,1024]{1,0:T(8,128)(2,1)S(1)}, u32[]{:S(2)}, u32[]{:S(2)}) %collective-permute-start) | collective-permute-done | bytes 524320 | tf_op jit(solution)/shard_map/ppermute | solution.py:199
  21.8 1.9 %collective-permute-start.7 = (bf16[256,1024]{1,0:T(8,128)(2,1)S(1)}, bf16[256,1024]{1,0:T(8,128)(2,1)S(1)}, u32[]{:S(2)}, u32[]{:S(2)}) collective-permute-start(bf16[256,1024]{1,0:T(8,128)(2,1)S(1)} %collective-permute-done.refs_6_), channel_id=1, source_target_pairs={{0,2},{1,3},{2,0},{3,1},{4,6},{5,7},{6,4},{7,5},{8,10},{9,11},{10,... | collective-permute-start | bytes 1572872 | tf_op jit(solution)/shard_map/ppermute | solution.py:199
  23.8 1.5 %collective-permute-start.6 = (bf16[256,512]{1,0:T(8,128)(2,1)S(1)}, bf16[256,512]{1,0:T(8,128)(2,1)S(1)}, u32[]{:S(2)}, u32[]{:S(2)}) collective-permute-start(bf16[256,512]{1,0:T(8,128)(2,1)S(1)} %collective-permute-done.3.refs_9_), channel_id=1, source_target_pairs={{2,8},{6,12},{10,16},{14,20},{18,24},{22,28},{26,32},{30,36},{34,4... | collective-permute-start | bytes 786440 | tf_op jit(solution)/shard_map/ppermute | solution.py:199
  25.2 0.1 collective-permute-start.5
  25.3 10.1 %collective-permute-start.4 = (bf16[256,512]{1,0:T(8,128)(2,1)S(1)}, bf16[256,512]{1,0:T(8,128)(2,1)S(1)}, u32[]{:S(2)}, u32[]{:S(2)}) collective-permute-start(bf16[256,512]{1,0:T(8,128)(2,1)S(1)} %collective-permute-done.3.refs_9_), channel_id=1, source_target_pairs={{0,4},{1,5},{2,6},{3,7},{4,8},{5,9},{6,10},{7,11},{8,12},{9,13},{1... | collective-permute-start | bytes 786440 | tf_op jit(solution)/shard_map/ppermute | solution.py:199
  35.4 22.2 %collective-permute-done.4.refs_10_ = bf16[256,512]{1,0:T(8,128)(2,1)S(1)} collective-permute-done((bf16[256,512]{1,0:T(8,128)(2,1)S(1)}, bf16[256,512]{1,0:T(8,128)(2,1)S(1)}, u32[]{:S(2)}, u32[]{:S(2)}) %collective-permute-start.4) | collective-permute-done | bytes 262176 | tf_op jit(solution)/shard_map/ppermute | solution.py:199
  57.7 0.1 collective-permute-start.13
  57.8 0.1 compare_select_fusion.refs_1_
  57.9 0.6 collective-permute-start.11
  58.5 2.0 %collective-permute-start.9 = (bf16[256,512]{1,0:T(8,128)(2,1)S(1)}, bf16[256,512]{1,0:T(8,128)(2,1)}, u32[]{:S(2)}, u32[]{:S(2)}) collective-permute-start(bf16[256,512]{1,0:T(8,128)(2,1)S(1)} %collective-permute-done.8.refs_9_), channel_id=1, source_target_pairs={{2,8},{6,12},{10,16},{14,20},{18,24},{22,28},{26,32},{30,36},{34,4... | collective-permute-start | bytes 786440 | tf_op jit(solution)/shard_map/ppermute | solution.py:199
  60.5 10.2 %collective-permute-done.10.refs_10_ = bf16[256,512]{1,0:T(8,128)(2,1)} collective-permute-done((bf16[256,512]{1,0:T(8,128)(2,1)S(1)}, bf16[256,512]{1,0:T(8,128)(2,1)}, u32[]{:S(2)}, u32[]{:S(2)}) %collective-permute-start.10) | collective-permute-done | bytes 262176 | tf_op jit(solution)/shard_map/ppermute | solution.py:199
  70.6 0.7 collective-permute-start.12
  71.4 0.7 subtract_add_fusion
  72.1 0.1 dynamic_update_slice.7.refs_0_
  72.3 1.5 %copy-done.1 = bf16[256,3584]{1,0:T(8,128)(2,1)S(1)} copy-done((bf16[256,3584]{1,0:T(8,128)(2,1)S(1)}, bf16[256,3584]{1,0:T(8,128)(2,1)}, u32[]{:S(2)}) %copy-start.1) | copy-done | bytes 1835032
  73.8 1.0 %copy-done.2 = bf16[256,1024]{1,0:T(8,128)(2,1)S(1)} copy-done((bf16[256,1024]{1,0:T(8,128)(2,1)S(1)}, bf16[256,1024]{1,0:T(8,128)(2,1)}, u32[]{:S(2)}) %copy-start.2) | copy-done | bytes 524312
  74.8 7.4 %attend.2.refs_13_ = bf16[256,3584]{1,0:T(8,128)(2,1)} custom-call(s32[3,16]{1,0:T(4,128)S(1)} %dynamic_update_slice.7.refs_0_, f32[2,128,128]{2,1,0:T(8,128)S(1)} %compare_select_fusion.refs_1_, bf16[256,3584]{1,0:T(8,128)(2,1)S(1)} %copy-done.1, bf16[128,1024]{1,0:T(8,128)(2,1)S(1)} %collective-permute-done.2.refs_3_, ...), custom_call_target="tpu_custom_call" | custom-call | flops 1879048192 | bytes 2097152 | tf_op jit(solution)/shard_map/attend/pallas_call | solution.py:171
  82.3 7.6 %attend.3 = bf16[256,3584]{1,0:T(8,128)(2,1)} custom-call(s32[3,16]{1,0:T(4,128)S(1)} %dynamic_update_slice.7.refs_0_, f32[2,128,128]{2,1,0:T(8,128)S(1)} %compare_select_fusion.refs_1_, bf16[256,3584]{1,0:T(8,128)(2,1)S(1)} %copy-done.1, bf16[128,1024]{1,0:T(8,128)(2,1)S(1)} %collective-permute-done.2.refs_3_, ...), custom_call_target="tpu_custom_call", output_to_operand_aliasing={{}: (13, {})} | custom-call | flops 1879048192 | bytes 2097152 | tf_op jit(solution)/shard_map/attend/pallas_call | solution.py:171
  (19 shorter events, 0.2 us)
Async XLA Ops:
  0.0 57.6 %copy-start = (s32[65536]{0:T(1024)S(1)}, s32[65536]{0:T(1024)}, u32[]{:S(2)}) copy-start(s32[65536]{0:T(1024)} %param.9) | copy-start | bytes 786436
  2.4 16.8 %collective-permute-start.1 = (bf16[256,1024]{1,0:T(8,128)(2,1)}, bf16[256,1024]{1,0:T(8,128)(2,1)S(1)}, u32[]{:S(2)}, u32[]{:S(2)}) collective-permute-start(bf16[256,1024]{1,0:T(8,128)(2,1)} %get-tuple-element.18.refs_5_), channel_id=1, source_target_pairs={{0,2},{1,3},{2,0},{3,1},{4,6},{5,7},{6,4},{7,5},{8,10},{9,11},{10,... | collective-permute-start | bytes 1572872 | tf_op jit(solution)/shard_map/ppermute | solution.py:199
  3.1 18.7 %collective-permute-start = (bf16[256,1024]{1,0:T(8,128)(2,1)}, bf16[256,1024]{1,0:T(8,128)(2,1)S(1)}, u32[]{:S(2)}, u32[]{:S(2)}) collective-permute-start(bf16[256,1024]{1,0:T(8,128)(2,1)} %get-tuple-element.18.refs_5_), channel_id=1, source_target_pairs={{0,4},{1,5},{2,6},{3,7},{4,8},{5,9},{6,10},{7,11},{8,12},{9,13},{1... | collective-permute-start | bytes 1572872 | tf_op jit(solution)/shard_map/ppermute | solution.py:199
  4.3 14.9 %collective-permute-start.2 = (bf16[128,1024]{1,0:T(8,128)(2,1)}, bf16[128,1024]{1,0:T(8,128)(2,1)S(1)}, u32[]{:S(2)}, u32[]{:S(2)}) collective-permute-start(bf16[128,1024]{1,0:T(8,128)(2,1)} %get-tuple-element.19), channel_id=1, source_target_pairs={{2,8},{3,9},{6,12},{7,13},{10,16},{11,17},{14,20},{15,21},{18,24},... | collective-permute-start | bytes 786440 | tf_op jit(solution)/shard_map/ppermute | solution.py:199
  8.8 14.9 %collective-permute-start.3 = (bf16[256,512]{1,0:T(8,128)(2,1)}, bf16[256,512]{1,0:T(8,128)(2,1)S(1)}, u32[]{:S(2)}, u32[]{:S(2)}) collective-permute-start(bf16[256,512]{1,0:T(8,128)(2,1)} %get-tuple-element.21), channel_id=1, source_target_pairs={{0,1},{1,0},{2,3},{3,2},{4,5},{5,4},{6,7},{7,6},{8,9},{9,8},{10,11... | collective-permute-start | bytes 786440 | tf_op jit(solution)/shard_map/ppermute | solution.py:199
  21.8 35.8 %collective-permute-start.7 = (bf16[256,1024]{1,0:T(8,128)(2,1)S(1)}, bf16[256,1024]{1,0:T(8,128)(2,1)S(1)}, u32[]{:S(2)}, u32[]{:S(2)}) collective-permute-start(bf16[256,1024]{1,0:T(8,128)(2,1)S(1)} %collective-permute-done.refs_6_), channel_id=1, source_target_pairs={{0,2},{1,3},{2,0},{3,1},{4,6},{5,7},{6,4},{7,5},{8,10},{9,11},{10,... | collective-permute-start | bytes 1572872 | tf_op jit(solution)/shard_map/ppermute | solution.py:199
  23.8 11.6 %collective-permute-start.6 = (bf16[256,512]{1,0:T(8,128)(2,1)S(1)}, bf16[256,512]{1,0:T(8,128)(2,1)S(1)}, u32[]{:S(2)}, u32[]{:S(2)}) collective-permute-start(bf16[256,512]{1,0:T(8,128)(2,1)S(1)} %collective-permute-done.3.refs_9_), channel_id=1, source_target_pairs={{2,8},{6,12},{10,16},{14,20},{18,24},{22,28},{26,32},{30,36},{34,4... | collective-permute-start | bytes 786440 | tf_op jit(solution)/shard_map/ppermute | solution.py:199
  25.2 10.2 %collective-permute-start.5 = (bf16[256,512]{1,0:T(8,128)(2,1)S(1)}, bf16[256,512]{1,0:T(8,128)(2,1)S(1)}, u32[]{:S(2)}, u32[]{:S(2)}) collective-permute-start(bf16[256,512]{1,0:T(8,128)(2,1)S(1)} %collective-permute-done.3.refs_9_), channel_id=1, source_target_pairs={{0,2},{1,3},{2,0},{3,1},{4,6},{5,7},{6,4},{7,5},{8,10},{9,11},{10,... | collective-permute-start | bytes 786440 | tf_op jit(solution)/shard_map/ppermute | solution.py:199
  25.3 32.3 %collective-permute-start.4 = (bf16[256,512]{1,0:T(8,128)(2,1)S(1)}, bf16[256,512]{1,0:T(8,128)(2,1)S(1)}, u32[]{:S(2)}, u32[]{:S(2)}) collective-permute-start(bf16[256,512]{1,0:T(8,128)(2,1)S(1)} %collective-permute-done.3.refs_9_), channel_id=1, source_target_pairs={{0,4},{1,5},{2,6},{3,7},{4,8},{5,9},{6,10},{7,11},{8,12},{9,13},{1... | collective-permute-start | bytes 786440 | tf_op jit(solution)/shard_map/ppermute | solution.py:199
  35.4 22.2 %collective-permute-start.8 = (bf16[256,512]{1,0:T(8,128)(2,1)}, bf16[256,512]{1,0:T(8,128)(2,1)S(1)}, u32[]{:S(2)}, u32[]{:S(2)}) collective-permute-start(bf16[256,512]{1,0:T(8,128)(2,1)} %get-tuple-element.25), channel_id=1, source_target_pairs={{0,1},{1,0},{2,3},{3,2},{4,5},{5,4},{6,7},{7,6},{8,9},{9,8},{10,11... | collective-permute-start | bytes 786440 | tf_op jit(solution)/shard_map/ppermute | solution.py:199
  57.6 13.0 %collective-permute-start.10 = (bf16[256,512]{1,0:T(8,128)(2,1)S(1)}, bf16[256,512]{1,0:T(8,128)(2,1)}, u32[]{:S(2)}, u32[]{:S(2)}) collective-permute-start(bf16[256,512]{1,0:T(8,128)(2,1)S(1)} %collective-permute-done.8.refs_9_), channel_id=1, source_target_pairs={{0,4},{1,5},{2,6},{3,7},{4,8},{5,9},{6,10},{7,11},{8,12},{9,13},{1... | collective-permute-start | bytes 786440 | tf_op jit(solution)/shard_map/ppermute | solution.py:199
  57.7 14.6 %collective-permute-start.13 = (bf16[256,512]{1,0:T(8,128)(2,1)S(1)}, bf16[256,512]{1,0:T(8,128)(2,1)}, u32[]{:S(2)}, u32[]{:S(2)}) collective-permute-start(bf16[256,512]{1,0:T(8,128)(2,1)S(1)} %collective-permute-done.4.refs_10_), channel_id=1, source_target_pairs={{0,2},{1,3},{2,0},{3,1},{4,6},{5,7},{6,4},{7,5},{8,10},{9,11},{10,... | collective-permute-start | bytes 786440 | tf_op jit(solution)/shard_map/ppermute | solution.py:199
  57.9 24.4 %collective-permute-start.11 = (bf16[256,512]{1,0:T(8,128)(2,1)S(1)}, bf16[256,512]{1,0:T(8,128)(2,1)}, u32[]{:S(2)}, u32[]{:S(2)}) collective-permute-start(bf16[256,512]{1,0:T(8,128)(2,1)S(1)} %collective-permute-done.8.refs_9_), channel_id=1, source_target_pairs={{0,2},{1,3},{2,0},{3,1},{4,6},{5,7},{6,4},{7,5},{8,10},{9,11},{10,... | collective-permute-start | bytes 786440 | tf_op jit(solution)/shard_map/ppermute | solution.py:199
  58.5 23.8 %collective-permute-start.9 = (bf16[256,512]{1,0:T(8,128)(2,1)S(1)}, bf16[256,512]{1,0:T(8,128)(2,1)}, u32[]{:S(2)}, u32[]{:S(2)}) collective-permute-start(bf16[256,512]{1,0:T(8,128)(2,1)S(1)} %collective-permute-done.8.refs_9_), channel_id=1, source_target_pairs={{2,8},{6,12},{10,16},{14,20},{18,24},{22,28},{26,32},{30,36},{34,4... | collective-permute-start | bytes 786440 | tf_op jit(solution)/shard_map/ppermute | solution.py:199
  70.6 11.6 %collective-permute-start.12 = (bf16[256,512]{1,0:T(8,128)(2,1)}, bf16[256,512]{1,0:T(8,128)(2,1)}, u32[]{:S(2)}, u32[]{:S(2)}) collective-permute-start(bf16[256,512]{1,0:T(8,128)(2,1)} %collective-permute-done.10.refs_10_), channel_id=1, source_target_pairs={{0,2},{1,3},{2,0},{3,1},{4,6},{5,7},{6,4},{7,5},{8,10},{9,11},{10,... | collective-permute-start | bytes 786440 | tf_op jit(solution)/shard_map/ppermute | solution.py:199
  72.3 1.5 %copy-start.1 = (bf16[256,3584]{1,0:T(8,128)(2,1)S(1)}, bf16[256,3584]{1,0:T(8,128)(2,1)}, u32[]{:S(2)}) copy-start(bf16[256,3584]{1,0:T(8,128)(2,1)} %refs_2_.3) | copy-start | bytes 5505028
  73.8 1.0 %copy-start.2 = (bf16[256,1024]{1,0:T(8,128)(2,1)S(1)}, bf16[256,1024]{1,0:T(8,128)(2,1)}, u32[]{:S(2)}) copy-start(bf16[256,1024]{1,0:T(8,128)(2,1)} %get-tuple-element.18.refs_5_) | copy-start | bytes 1572868
where the time goes:
time: 90.2 us; the launch traced here: 89.9 us
  waiting for transfers between devices  41.1 us (46%)
  starting transfers between devices  27.6 us (31%)
  Pallas kernels  17.5 us (19%)
  local copies, waits for them, and re-layouts  2.83 us (3%)
    ppermute x14, waiting for transfers between devices, move(): return lax.ppermute(value, AXES, pairs)  41.1 us
    ppermute x14, starting transfers between devices, move(): return lax.ppermute(value, AXES, pairs)  27.6 us
    pallas_call x2, Pallas kernels, attend(): pl.pallas_call(lambda *refs: attend_kernel(heads, first_head, *refs), gri...  15.1 us
    unnamed x6, local copies, waits for them, and re-layouts  2.54 us
    pallas_call x1, Pallas kernels, pack(): pl.pallas_call(pack_kernel, out_shape=[jax.ShapeDtypeStruct(shape, jnp.bf...  2.39 us
  transfers between devices with their start and end apart: 14, of which 4 were waited for; matrix products, arithmetic and copies ran while one was open for 1% of the time, Pallas kernels for 8%

commit v1 on v0

v1 whole, which is shorter than its diff:
```python
import math

import jax
import jax.numpy as jnp
from jax import lax
from jax.experimental import pallas as pl
from jax.experimental.pallas import tpu as pltpu
from jax.sharding import PartitionSpec as P

QUERY_HEADS = 28
KEY_VALUE_HEADS = 4
GROUP = QUERY_HEADS // KEY_VALUE_HEADS
HEAD_SIZE = 128
PAIR = 2 * HEAD_SIZE
TILE = 128
TOKENS = 256
KEPT = 8
REACH = 6
AXES = ("blk", "head")
HEAD_GROUPS = ((0, 2), (2, 2))
SCALE = math.log2(math.e) / math.sqrt(HEAD_SIZE)
NEVER = -1e30


def pack_kernel(keys, values, own, *parts):
    for (first, count), target in zip(((0, KEY_VALUE_HEADS),), (own, *parts)):
        for head in range(count):
            columns = pl.ds((first + head) * HEAD_SIZE, HEAD_SIZE)
            target[:, pl.ds(head * PAIR, HEAD_SIZE)] = keys[:, columns]
            target[:, pl.ds(head * PAIR + HEAD_SIZE, HEAD_SIZE)] = values[:, columns]


def pack(keys, values):
    whole = pl.BlockSpec(memory_space=pltpu.VMEM)
    widths = [KEY_VALUE_HEADS * PAIR]
    return pl.pallas_call(
        pack_kernel,
        out_shape=[pltpu.VMEM((TOKENS, width), jnp.bfloat16) for width in widths],
        in_specs=[whole, whole],
        out_specs=[whole] * len(widths),
        name="pack",
    )(keys, values)


def attend_kernel(first_head, heads, kept, bias, queries, *refs):
    blocks = refs[: REACH + 1]
    out, q, rows_kept, keys, values, kept_keys, kept_values, arrived = refs[-8:]
    blk = lax.axis_index("blk")
    half = lax.axis_index("head")
    width = heads * GROUP * HEAD_SIZE
    first = first_head * GROUP * HEAD_SIZE
    listed = pltpu.make_async_copy(kept, rows_kept, arrived.at[0])
    listed.start()
    fetch = pltpu.make_async_copy(queries.at[:, pl.ds(first, width)], q, arrived.at[1])
    fetch.start()
    origin = (blk * 2 + half - REACH) * (TOKENS // TILE)

    def gather(head):
        for behind, block in enumerate(blocks):
            skip = TOKENS - block.shape[0]
            rows = pl.ds((REACH - behind) * TOKENS + skip, block.shape[0])
            keys[head, rows, :] = block[:, pl.ds(head * PAIR, HEAD_SIZE)]
            values[head, rows, :] = block[:, pl.ds(head * PAIR + HEAD_SIZE, HEAD_SIZE)]
        if head == 0:
            listed.wait()
        for tile in range(2):
            entries = [rows_kept[half * 2 + tile, entry] - origin for entry in range(KEPT)]
            for entry, index in enumerate(entries):
                rows = pl.ds(pl.multiple_of(index * TILE, TILE), TILE)
                slot = pl.ds(entry * TILE, TILE)
                key = keys[head, rows, :]
                value = values[head, rows, :]
                count = jnp.float32(1.0)
                if entry:
                    again = index == entries[0]
                    key = jnp.where(again, jnp.broadcast_to(key[0:1, :], key.shape), key)
                    for earlier in entries[1:entry]:
                        again = again | (index == earlier)
                    value = jnp.where(again, jnp.zeros_like(value), value)
                    count = jnp.where(again, 0.0, 1.0)
                kept_keys[head, tile, slot, :] = key
                kept_values[head, tile, slot, :HEAD_SIZE] = value
                kept_values[head, tile, slot, HEAD_SIZE:] = jnp.full(
                    value.shape, count.astype(jnp.bfloat16)
                )

    for head in range(heads):
        gather(head)
        if head == 0:
            fetch.wait()
        for tile in range(2):
            for member in range(GROUP):
                rows = pl.ds(tile * TILE, TILE)
                columns = pl.ds((head * GROUP + member) * HEAD_SIZE, HEAD_SIZE)
                scores = lax.dot_general(
                    q[rows, columns],
                    kept_keys[head, tile],
                    (((1,), (1,)), ((), ())),
                    preferred_element_type=jnp.float32,
                )
                scores = jnp.concatenate(
                    [scores[:, :TILE] + bias[tile], scores[:, TILE:]], axis=1
                )
                top = jnp.max(scores, axis=1, keepdims=True)
                weights = jnp.exp2((scores - top) * SCALE).astype(jnp.bfloat16)
                summed = jnp.dot(
                    weights, kept_values[head, tile], preferred_element_type=jnp.float32
                )
                result = summed[:, :HEAD_SIZE] / summed[:, HEAD_SIZE:]
                out[rows, columns] = result.astype(jnp.bfloat16)


def attend(group, kept, bias, queries, blocks, previous):
    first_head, heads = group
    width = heads * GROUP * HEAD_SIZE
    part = heads * PAIR
    number = first_head // heads
    whole = pl.BlockSpec(memory_space=pltpu.VMEM)
    queries = pltpu.with_memory_space_constraint(queries, pltpu.HBM)
    kept = pltpu.with_memory_space_constraint(kept, pltpu.HBM)
    operands = [kept, bias, queries, *blocks]
    specs = [
        pl.BlockSpec(memory_space=pltpu.HBM),
        whole,
        pl.BlockSpec(memory_space=pltpu.HBM),
    ]
    for block in blocks:
        if block.shape[1] == part:
            specs.append(whole)
        else:
            specs.append(pl.BlockSpec((block.shape[0], part), lambda i: (0, number)))
    aliases = {}
    if previous is not None:
        aliases = {len(operands): 0}
        operands.append(previous)
        specs.append(pl.BlockSpec(memory_space=pl.ANY))
    return pl.pallas_call(
        lambda *refs: attend_kernel(first_head, heads, *refs),
        grid=(1,),
        out_shape=jax.ShapeDtypeStruct(queries.shape, jnp.bfloat16),
        in_specs=specs,
        out_specs=pl.BlockSpec((TOKENS, width), lambda i: (0, number)),
        scratch_shapes=[
            pltpu.VMEM((TOKENS, width), jnp.bfloat16),
            pltpu.SMEM((2 * 2, KEPT), jnp.int32),
            pltpu.VMEM((heads, (REACH + 1) * TOKENS, HEAD_SIZE), jnp.bfloat16),
            pltpu.VMEM((heads, (REACH + 1) * TOKENS, HEAD_SIZE), jnp.bfloat16),
            pltpu.VMEM((heads, 2, KEPT * TILE, HEAD_SIZE), jnp.bfloat16),
            pltpu.VMEM((heads, 2, KEPT * TILE, 2 * HEAD_SIZE), jnp.bfloat16),
            pltpu.SemaphoreType.DMA((2,)),
        ],
        input_output_aliases=aliases,
        compiler_params=pltpu.CompilerParams(vmem_limit_bytes=32 * 2**20),
        cost_estimate=pl.CostEstimate(flops=2**20, bytes_accessed=2**16, transcendentals=0),
        name="attend",
    )(*operands)


def shards(queries, keys, values, kept, frame_ids):
    blk = lax.axis_index("blk")
    half = lax.axis_index("head")
    devices = lax.axis_size("blk") * 2

    def ahead(value, blocks):
        pairs = [(source, (source + blocks) % devices) for source in range(devices)]
        return lax.ppermute(value, AXES, pairs)

    tokens = lax.dynamic_slice_in_dim(frame_ids, (blk * 2 + half) * TOKENS, TOKENS, 0)
    frames = tokens.reshape(2, TILE)
    bias = jnp.where(frames[:, None, :] <= frames[:, :, None], 0.0, NEVER).astype(jnp.float32)

    (own,) = pack(keys, values)
    both_1 = ahead(own, 1)
    both_2 = ahead(own, 2)
    both_4 = ahead(both_2, 2)
    both_1, bias = lax.optimization_barrier((both_1, bias))
    width = HEAD_GROUPS[0][1] * PAIR
    first_3 = ahead(both_1[:, :width], 2)
    second_3 = ahead(both_1[:, width:], 2)
    both_6 = ahead(both_4[TILE:], 2)
    first_3, second_3 = lax.optimization_barrier((first_3, second_3))
    first_5 = ahead(first_3, 2)
    both_6, first_5 = lax.optimization_barrier((both_6, first_5))
    second_5 = ahead(second_3, 2)
    blocks = (own, both_1, both_2, first_3, both_4, first_5, both_6)
    result = attend(HEAD_GROUPS[0], kept, bias, queries, blocks, None)
    second_5, result = lax.optimization_barrier((second_5, result))
    blocks = (own, both_1, both_2, second_3, both_4, second_5, both_6)
    return attend(HEAD_GROUPS[1], kept, bias, queries, blocks, result)


def solution(mesh):
    placed = (
        P(AXES, None),
        P(AXES, None),
        P(AXES, None),
        P("blk", None),
        P(),
    )
    return jax.shard_map(
        shards, mesh=mesh, in_specs=placed, out_specs=P(AXES, None), check_vma=False
    )
```

time: 90.2 us -> 84.7 us (0.939)
  the two profiles are of different devices: /device:TPU:121 before, /device:TPU:0 now
where the time goes in v1:
time: 84.7 us; the launch traced here: 84.5 us
  waiting for transfers between devices  62.2 us (73%)
  Pallas kernels  15.7 us (19%)
  starting transfers between devices  6.14 us (7%)
    ppermute x8, waiting for transfers between devices, ahead(): return lax.ppermute(value, AXES, pairs)  62.2 us
    pallas_call x2, Pallas kernels, attend(): pl.pallas_call(lambda *refs: attend_kernel(first_head, heads, *refs), gri...  14.5 us
    ppermute x8, starting transfers between devices, ahead(): return lax.ppermute(value, AXES, pairs)  6.14 us
  transfers between devices with their start and end apart: 8, of which 5 were waited for; matrix products, arithmetic and copies ran while one was open for 0% of the time, Pallas kernels for 9%

profile of v1, /device:TPU:0, one launch (start us, length us, event | category | flops | bytes accessed | tf_op | source)
XLA Modules:
  0.0 84.5 jit_solution(8189190205313358022)
XLA Ops:
  0.0 0.0 copy-start
  0.0 1.2 %pack.1.refs_3_ = bf16[256,1024]{1,0:T(8,128)(2,1)S(1)} custom-call(bf16[256,512]{1,0:T(8,128)(2,1)} %keys.1, bf16[256,512]{1,0:T(8,128)(2,1)} %values.1), custom_call_target="tpu_custom_call" | custom-call | tf_op jit(solution)/shard_map/pack/pallas_call | solution.py:36
  1.2 0.1 collective-permute-start.1
  1.3 5.5 %collective-permute-start = (bf16[256,1024]{1,0:T(8,128)(2,1)S(1)}, bf16[256,1024]{1,0:T(8,128)(2,1)S(1)}, u32[]{:S(2)}, u32[]{:S(2)}) collective-permute-start(bf16[256,1024]{1,0:T(8,128)(2,1)S(1)} %pack.1.refs_3_), channel_id=1, source_target_pairs={{0,1},{1,2},{2,3},{3,4},{4,5},{5,6},{6,7},{7,8},{8,9},{9,10},{10,1... | collective-permute-start | bytes 1572872 | tf_op jit(solution)/shard_map/ppermute | solution.py:166
  6.8 0.0 copy-done
  6.8 0.1 dynamic-slice_bitcast_fusion
  6.9 27.8 %collective-permute-done.1.refs_5_ = bf16[256,1024]{1,0:T(8,128)(2,1)S(1)} collective-permute-done((bf16[256,1024]{1,0:T(8,128)(2,1)S(1)}, bf16[256,1024]{1,0:T(8,128)(2,1)S(1)}, u32[]{:S(2)}, u32[]{:S(2)}) %collective-permute-start.1) | collective-permute-done | bytes 524320 | tf_op jit(solution)/shard_map/ppermute | solution.py:166
  34.8 0.0 collective-permute-start.4
  34.8 0.1 compare_select_fusion.refs_1_
  34.9 0.0 collective-permute-done.refs_4_
  34.9 0.1 collective-permute-start.3
  35.0 0.1 collective-permute-start.2
  35.1 17.3 %collective-permute-done.3.refs_6_ = bf16[256,512]{1,0:T(8,128)(2,1)S(1)} collective-permute-done((bf16[256,512]{1,0:T(8,128)(2,1)S(1)}, bf16[256,512]{1,0:T(8,128)(2,1)S(1)}, u32[]{:S(2)}, u32[]{:S(2)}) %collective-permute-start.3) | collective-permute-done | bytes 262176 | tf_op jit(solution)/shard_map/ppermute | solution.py:166
  52.4 2.8 %collective-permute-done.2.refs_6_ = bf16[256,512]{1,0:T(8,128)(2,1)S(1)} collective-permute-done((bf16[256,512]{1,0:T(8,128)(2,1)S(1)}, bf16[256,512]{1,0:T(8,128)(2,1)S(1)}, u32[]{:S(2)}, u32[]{:S(2)}) %collective-permute-start.2) | collective-permute-done | bytes 262176 | tf_op jit(solution)/shard_map/ppermute | solution.py:166
  55.2 0.0 collective-permute-start.7
  55.2 0.0 collective-permute-done.4.refs_7_
  55.3 0.1 collective-permute-start.6
  55.4 0.3 collective-permute-start.5
  55.6 11.4 %collective-permute-done.7.refs_8_ = bf16[256,512]{1,0:T(8,128)(2,1)S(1)} collective-permute-done((bf16[256,512]{1,0:T(8,128)(2,1)S(1)}, bf16[256,512]{1,0:T(8,128)(2,1)S(1)}, u32[]{:S(2)}, u32[]{:S(2)}) %collective-permute-start.7) | collective-permute-done | bytes 262176 | tf_op jit(solution)/shard_map/ppermute | solution.py:166
  67.1 2.8 %collective-permute-done.6.refs_9_ = bf16[128,1024]{1,0:T(8,128)(2,1)S(1)} collective-permute-done((bf16[128,1024]{1,0:T(8,128)(2,1)S(1)}, bf16[128,1024]{1,0:T(8,128)(2,1)S(1)}, u32[]{:S(2)}, u32[]{:S(2)}) %collective-permute-start.6) | collective-permute-done | bytes 262176 | tf_op jit(solution)/shard_map/ppermute | solution.py:166
  69.9 7.2 %attend.2.refs_10_ = bf16[256,3584]{1,0:T(8,128)(2,1)} custom-call(s32[4,8]{1,0:T(4,128)} %refs_0_.3, f32[2,128,128]{2,1,0:T(8,128)S(1)} %compare_select_fusion.refs_1_, bf16[256,3584]{1,0:T(8,128)(2,1)} %refs_2_.3, bf16[256,1024]{1,0:T(8,128)(2,1)S(1)} %pack.1.refs_3_, bf16[256,1024]{1,0:T(8,128)(2,1)S(1)} %collective-permute-done.refs_4_, ...), custom_call_target="tpu_custom_call" | custom-call | flops 1048576 | bytes 65536 | tf_op jit(solution)/shard_map/attend/pallas_call | solution.py:137
  77.1 0.0 collective-permute-done.5.refs_8_
  77.1 7.2 %attend.3 = bf16[256,3584]{1,0:T(8,128)(2,1)} custom-call(s32[4,8]{1,0:T(4,128)} %refs_0_.3, f32[2,128,128]{2,1,0:T(8,128)S(1)} %compare_select_fusion.refs_1_, bf16[256,3584]{1,0:T(8,128)(2,1)} %refs_2_.3, bf16[256,1024]{1,0:T(8,128)(2,1)S(1)} %pack.1.refs_3_, bf16[256,1024]{1,0:T(8,128)(2,1)S(1)} %collective-permute-done.refs_4_, ...), custom_call_target="tpu_custom_call", output_to_operand_aliasing={{}: (10, {})} | custom-call | flops 1048576 | bytes 65536 | tf_op jit(solution)/shard_map/attend/pallas_call | solution.py:137
  (2 shorter events, 0.1 us)
Async XLA Ops:
  0.0 6.8 %copy-start = (s32[65536]{0:T(1024)S(1)}, s32[65536]{0:T(1024)}, u32[]{:S(2)}) copy-start(s32[65536]{0:T(1024)} %param.9) | copy-start | bytes 786436
  1.2 33.5 %collective-permute-start.1 = (bf16[256,1024]{1,0:T(8,128)(2,1)S(1)}, bf16[256,1024]{1,0:T(8,128)(2,1)S(1)}, u32[]{:S(2)}, u32[]{:S(2)}) collective-permute-start(bf16[256,1024]{1,0:T(8,128)(2,1)S(1)} %pack.1.refs_3_), channel_id=1, source_target_pairs={{0,2},{1,3},{2,4},{3,5},{4,6},{5,7},{6,8},{7,9},{8,10},{9,11},{10,... | collective-permute-start | bytes 1572872 | tf_op jit(solution)/shard_map/ppermute | solution.py:166
  1.3 33.6 %collective-permute-start = (bf16[256,1024]{1,0:T(8,128)(2,1)S(1)}, bf16[256,1024]{1,0:T(8,128)(2,1)S(1)}, u32[]{:S(2)}, u32[]{:S(2)}) collective-permute-start(bf16[256,1024]{1,0:T(8,128)(2,1)S(1)} %pack.1.refs_3_), channel_id=1, source_target_pairs={{0,1},{1,2},{2,3},{3,4},{4,5},{5,6},{6,7},{7,8},{8,9},{9,10},{10,1... | collective-permute-start | bytes 1572872 | tf_op jit(solution)/shard_map/ppermute | solution.py:166
  34.8 20.5 %collective-permute-start.4 = (bf16[256,1024]{1,0:T(8,128)(2,1)S(1)}, bf16[256,1024]{1,0:T(8,128)(2,1)S(1)}, u32[]{:S(2)}, u32[]{:S(2)}) collective-permute-start(bf16[256,1024]{1,0:T(8,128)(2,1)S(1)} %collective-permute-done.1.refs_5_), channel_id=1, source_target_pairs={{0,2},{1,3},{2,4},{3,5},{4,6},{5,7},{6,8},{7,9},{8,10},{9,11},{10,... | collective-permute-start | bytes 1572872 | tf_op jit(solution)/shard_map/ppermute | solution.py:166
  34.9 17.5 %collective-permute-start.3 = (bf16[256,512]{1,0:T(8,128)(2,1)S(1)}, bf16[256,512]{1,0:T(8,128)(2,1)S(1)}, u32[]{:S(2)}, u32[]{:S(2)}) collective-permute-start(bf16[256,512]{1,0:T(8,128)(2,1)S(1)} %get-tuple-element.21), channel_id=1, source_target_pairs={{0,2},{1,3},{2,4},{3,5},{4,6},{5,7},{6,8},{7,9},{8,10},{9,11},{10,... | collective-permute-start | bytes 786440 | tf_op jit(solution)/shard_map/ppermute | solution.py:166
  35.0 20.2 %collective-permute-start.2 = (bf16[256,512]{1,0:T(8,128)(2,1)S(1)}, bf16[256,512]{1,0:T(8,128)(2,1)S(1)}, u32[]{:S(2)}, u32[]{:S(2)}) collective-permute-start(bf16[256,512]{1,0:T(8,128)(2,1)S(1)} %get-tuple-element.22), channel_id=1, source_target_pairs={{0,2},{1,3},{2,4},{3,5},{4,6},{5,7},{6,8},{7,9},{8,10},{9,11},{10,... | collective-permute-start | bytes 786440 | tf_op jit(solution)/shard_map/ppermute | solution.py:166
  55.2 11.8 %collective-permute-start.7 = (bf16[256,512]{1,0:T(8,128)(2,1)S(1)}, bf16[256,512]{1,0:T(8,128)(2,1)S(1)}, u32[]{:S(2)}, u32[]{:S(2)}) collective-permute-start(bf16[256,512]{1,0:T(8,128)(2,1)S(1)} %collective-permute-done.2.refs_6_), channel_id=1, source_target_pairs={{0,2},{1,3},{2,4},{3,5},{4,6},{5,7},{6,8},{7,9},{8,10},{9,11},{10,... | collective-permute-start | bytes 786440 | tf_op jit(solution)/shard_map/ppermute | solution.py:166
  55.3 14.6 %collective-permute-start.6 = (bf16[128,1024]{1,0:T(8,128)(2,1)S(1)}, bf16[128,1024]{1,0:T(8,128)(2,1)S(1)}, u32[]{:S(2)}, u32[]{:S(2)}) collective-permute-start(bf16[128,1024]{1,0:T(8,128)(2,1)S(1)} %slice.12), channel_id=1, source_target_pairs={{0,2},{1,3},{2,4},{3,5},{4,6},{5,7},{6,8},{7,9},{8,10},{9,11},{10,... | collective-permute-start | bytes 786440 | tf_op jit(solution)/shard_map/ppermute | solution.py:166
  55.4 21.7 %collective-permute-start.5 = (bf16[256,512]{1,0:T(8,128)(2,1)S(1)}, bf16[256,512]{1,0:T(8,128)(2,1)S(1)}, u32[]{:S(2)}, u32[]{:S(2)}) collective-permute-start(bf16[256,512]{1,0:T(8,128)(2,1)S(1)} %collective-permute-done.3.refs_6_), channel_id=1, source_target_pairs={{0,2},{1,3},{2,4},{3,5},{4,6},{5,7},{6,8},{7,9},{8,10},{9,11},{10,... | collective-permute-start | bytes 786440 | tf_op jit(solution)/shard_map/ppermute | solution.py:166

commit v2 on v1

--- a/solution.py
+++ b/solution.py
@@ -161,8 +161,12 @@
     half = lax.axis_index("head")
     devices = lax.axis_size("blk") * 2
 
-    def ahead(value, blocks):
-        pairs = [(source, (source + blocks) % devices) for source in range(devices)]
+    def ahead(value, blocks, spare=()):
+        first = blocks + len(spare)
+        pairs = [(target - blocks, target) for target in range(first, devices)]
+        around = [target for target in range(first) if target not in spare]
+        pairs += [(devices - blocks + i, target) for i, target in enumerate(around)]
+        pairs += list(enumerate(spare))
         return lax.ppermute(value, AXES, pairs)
 
     tokens = lax.dynamic_slice_in_dim(frame_ids, (blk * 2 + half) * TOKENS, TOKENS, 0)
@@ -172,16 +176,16 @@
     (own,) = pack(keys, values)
     both_1 = ahead(own, 1)
     both_2 = ahead(own, 2)
-    both_4 = ahead(both_2, 2)
+    both_4 = ahead(both_2, 2, (1, 0))
     both_1, bias = lax.optimization_barrier((both_1, bias))
     width = HEAD_GROUPS[0][1] * PAIR
-    first_3 = ahead(both_1[:, :width], 2)
-    second_3 = ahead(both_1[:, width:], 2)
-    both_6 = ahead(both_4[TILE:], 2)
+    first_3 = ahead(both_1[:, :width], 2, (2,))
+    second_3 = ahead(both_1[:, width:], 2, (2,))
+    both_6 = ahead(both_4[TILE:], 2, (2, 3, 0, 1))
     first_3, second_3 = lax.optimization_barrier((first_3, second_3))
-    first_5 = ahead(first_3, 2)
+    first_5 = ahead(first_3, 2, (2, 3, 0))
     both_6, first_5 = lax.optimization_barrier((both_6, first_5))
-    second_5 = ahead(second_3, 2)
+    second_5 = ahead(second_3, 2, (2, 3, 0))
     blocks = (own, both_1, both_2, first_3, both_4, first_5, both_6)
     result = attend(HEAD_GROUPS[0], kept, bias, queries, blocks, None)
     second_5, result = lax.optimization_barrier((second_5, result))

time: 84.7 us -> 82.2 us (0.970)
  the two profiles are of different devices: /device:TPU:0 before, /device:TPU:16 now
where the time goes in v2:
time: 82.2 us; the launch traced here: 82.1 us
  waiting for transfers between devices  55.4 us (67%)
  Pallas kernels  15.7 us (19%)
  starting transfers between devices  10.6 us (13%)
    ppermute x8, waiting for transfers between devices, ahead(): return lax.ppermute(value, AXES, pairs)  55.4 us
    pallas_call x2, Pallas kernels, attend(): pl.pallas_call(lambda *refs: attend_kernel(first_head, heads, *refs), gri...  14.5 us
    ppermute x8, starting transfers between devices, ahead(): return lax.ppermute(value, AXES, pairs)  10.6 us
  transfers between devices with their start and end apart: 8, of which 6 were waited for; matrix products, arithmetic and copies ran while one was open for 0% of the time, Pallas kernels for 9%

profile of v2, /device:TPU:16, one launch (start us, length us, event | category | flops | bytes accessed | tf_op | source)
XLA Modules:
  0.0 82.1 jit_solution(9439382686843537542)
XLA Ops:
  0.0 0.0 copy-start
  0.0 1.2 %pack.1.refs_3_ = bf16[256,1024]{1,0:T(8,128)(2,1)S(1)} custom-call(bf16[256,512]{1,0:T(8,128)(2,1)} %keys.1, bf16[256,512]{1,0:T(8,128)(2,1)} %values.1), custom_call_target="tpu_custom_call" | custom-call | tf_op jit(solution)/shard_map/pack/pallas_call | solution.py:36
  1.2 0.1 collective-permute-start.1
  1.3 7.3 %collective-permute-start = (bf16[256,1024]{1,0:T(8,128)(2,1)S(1)}, bf16[256,1024]{1,0:T(8,128)(2,1)S(1)}, u32[]{:S(2)}, u32[]{:S(2)}) collective-permute-start(bf16[256,1024]{1,0:T(8,128)(2,1)S(1)} %pack.1.refs_3_), channel_id=1, source_target_pairs={{0,1},{1,2},{2,3},{3,4},{4,5},{5,6},{6,7},{7,8},{8,9},{9,10},{10,1... | collective-permute-start | bytes 1572872 | tf_op jit(solution)/shard_map/ppermute | solution.py:170
  8.6 0.0 copy-done
  8.6 0.1 dynamic-slice_bitcast_fusion
  8.7 11.2 %collective-permute-done.1.refs_5_ = bf16[256,1024]{1,0:T(8,128)(2,1)S(1)} collective-permute-done((bf16[256,1024]{1,0:T(8,128)(2,1)S(1)}, bf16[256,1024]{1,0:T(8,128)(2,1)S(1)}, u32[]{:S(2)}, u32[]{:S(2)}) %collective-permute-start.1) | collective-permute-done | bytes 524320 | tf_op jit(solution)/shard_map/ppermute | solution.py:170
  19.9 0.0 collective-permute-start.4
  19.9 0.1 compare_select_fusion.refs_1_
  20.0 9.5 %collective-permute-done.refs_4_ = bf16[256,1024]{1,0:T(8,128)(2,1)S(1)} collective-permute-done((bf16[256,1024]{1,0:T(8,128)(2,1)S(1)}, bf16[256,1024]{1,0:T(8,128)(2,1)S(1)}, u32[]{:S(2)}, u32[]{:S(2)}) %collective-permute-start) | collective-permute-done | bytes 524320 | tf_op jit(solution)/shard_map/ppermute | solution.py:170
  29.6 2.8 %collective-permute-start.3 = (bf16[256,512]{1,0:T(8,128)(2,1)S(1)}, bf16[256,512]{1,0:T(8,128)(2,1)S(1)}, u32[]{:S(2)}, u32[]{:S(2)}) collective-permute-start(bf16[256,512]{1,0:T(8,128)(2,1)S(1)} %get-tuple-element.21), channel_id=1, source_target_pairs={{1,3},{2,4},{3,5},{4,6},{5,7},{6,8},{7,9},{8,10},{9,11},{10,12},{1... | collective-permute-start | bytes 786440 | tf_op jit(solution)/shard_map/ppermute | solution.py:170
  32.4 0.1 collective-permute-start.2
  32.4 18.8 %collective-permute-done.3.refs_6_ = bf16[256,512]{1,0:T(8,128)(2,1)S(1)} collective-permute-done((bf16[256,512]{1,0:T(8,128)(2,1)S(1)}, bf16[256,512]{1,0:T(8,128)(2,1)S(1)}, u32[]{:S(2)}, u32[]{:S(2)}) %collective-permute-start.3) | collective-permute-done | bytes 262176 | tf_op jit(solution)/shard_map/ppermute | solution.py:170
  51.2 2.8 %collective-permute-done.2.refs_6_ = bf16[256,512]{1,0:T(8,128)(2,1)S(1)} collective-permute-done((bf16[256,512]{1,0:T(8,128)(2,1)S(1)}, bf16[256,512]{1,0:T(8,128)(2,1)S(1)}, u32[]{:S(2)}, u32[]{:S(2)}) %collective-permute-start.2) | collective-permute-done | bytes 262176 | tf_op jit(solution)/shard_map/ppermute | solution.py:170
  54.0 0.0 collective-permute-start.7
  54.0 0.0 collective-permute-done.4.refs_7_
  54.1 0.1 collective-permute-start.6
  54.2 0.3 collective-permute-start.5
  54.4 10.2 %collective-permute-done.7.refs_8_ = bf16[256,512]{1,0:T(8,128)(2,1)S(1)} collective-permute-done((bf16[256,512]{1,0:T(8,128)(2,1)S(1)}, bf16[256,512]{1,0:T(8,128)(2,1)S(1)}, u32[]{:S(2)}, u32[]{:S(2)}) %collective-permute-start.7) | collective-permute-done | bytes 262176 | tf_op jit(solution)/shard_map/ppermute | solution.py:170
  64.6 2.8 %collective-permute-done.6.refs_9_ = bf16[128,1024]{1,0:T(8,128)(2,1)S(1)} collective-permute-done((bf16[128,1024]{1,0:T(8,128)(2,1)S(1)}, bf16[128,1024]{1,0:T(8,128)(2,1)S(1)}, u32[]{:S(2)}, u32[]{:S(2)}) %collective-permute-start.6) | collective-permute-done | bytes 262176 | tf_op jit(solution)/shard_map/ppermute | solution.py:170
  67.4 7.2 %attend.2.refs_10_ = bf16[256,3584]{1,0:T(8,128)(2,1)} custom-call(s32[4,8]{1,0:T(4,128)} %refs_0_.3, f32[2,128,128]{2,1,0:T(8,128)S(1)} %compare_select_fusion.refs_1_, bf16[256,3584]{1,0:T(8,128)(2,1)} %refs_2_.3, bf16[256,1024]{1,0:T(8,128)(2,1)S(1)} %pack.1.refs_3_, bf16[256,1024]{1,0:T(8,128)(2,1)S(1)} %collective-permute-done.refs_4_, ...), custom_call_target="tpu_custom_call" | custom-call | flops 1048576 | bytes 65536 | tf_op jit(solution)/shard_map/attend/pallas_call | solution.py:137
  74.7 0.0 collective-permute-done.5.refs_8_
  74.7 7.2 %attend.3 = bf16[256,3584]{1,0:T(8,128)(2,1)} custom-call(s32[4,8]{1,0:T(4,128)} %refs_0_.3, f32[2,128,128]{2,1,0:T(8,128)S(1)} %compare_select_fusion.refs_1_, bf16[256,3584]{1,0:T(8,128)(2,1)} %refs_2_.3, bf16[256,1024]{1,0:T(8,128)(2,1)S(1)} %pack.1.refs_3_, bf16[256,1024]{1,0:T(8,128)(2,1)S(1)} %collective-permute-done.refs_4_, ...), custom_call_target="tpu_custom_call", output_to_operand_aliasing={{}: (10, {})} | custom-call | flops 1048576 | bytes 65536 | tf_op jit(solution)/shard_map/attend/pallas_call | solution.py:137
  (2 shorter events, 0.1 us)
Async XLA Ops:
  0.0 8.6 %copy-start = (s32[65536]{0:T(1024)S(1)}, s32[65536]{0:T(1024)}, u32[]{:S(2)}) copy-start(s32[65536]{0:T(1024)} %param.9) | copy-start | bytes 786436
  1.2 18.7 %collective-permute-start.1 = (bf16[256,1024]{1,0:T(8,128)(2,1)S(1)}, bf16[256,1024]{1,0:T(8,128)(2,1)S(1)}, u32[]{:S(2)}, u32[]{:S(2)}) collective-permute-start(bf16[256,1024]{1,0:T(8,128)(2,1)S(1)} %pack.1.refs_3_), channel_id=1, source_target_pairs={{0,2},{1,3},{2,4},{3,5},{4,6},{5,7},{6,8},{7,9},{8,10},{9,11},{10,... | collective-permute-start | bytes 1572872 | tf_op jit(solution)/shard_map/ppermute | solution.py:170
  1.3 28.2 %collective-permute-start = (bf16[256,1024]{1,0:T(8,128)(2,1)S(1)}, bf16[256,1024]{1,0:T(8,128)(2,1)S(1)}, u32[]{:S(2)}, u32[]{:S(2)}) collective-permute-start(bf16[256,1024]{1,0:T(8,128)(2,1)S(1)} %pack.1.refs_3_), channel_id=1, source_target_pairs={{0,1},{1,2},{2,3},{3,4},{4,5},{5,6},{6,7},{7,8},{8,9},{9,10},{10,1... | collective-permute-start | bytes 1572872 | tf_op jit(solution)/shard_map/ppermute | solution.py:170
  19.9 34.1 %collective-permute-start.4 = (bf16[256,1024]{1,0:T(8,128)(2,1)S(1)}, bf16[256,1024]{1,0:T(8,128)(2,1)S(1)}, u32[]{:S(2)}, u32[]{:S(2)}) collective-permute-start(bf16[256,1024]{1,0:T(8,128)(2,1)S(1)} %collective-permute-done.1.refs_5_), channel_id=1, source_target_pairs={{2,4},{3,5},{4,6},{5,7},{6,8},{7,9},{8,10},{9,11},{10,12},{11,13},... | collective-permute-start | bytes 1572872 | tf_op jit(solution)/shard_map/ppermute | solution.py:170
  29.6 21.6 %collective-permute-start.3 = (bf16[256,512]{1,0:T(8,128)(2,1)S(1)}, bf16[256,512]{1,0:T(8,128)(2,1)S(1)}, u32[]{:S(2)}, u32[]{:S(2)}) collective-permute-start(bf16[256,512]{1,0:T(8,128)(2,1)S(1)} %get-tuple-element.21), channel_id=1, source_target_pairs={{1,3},{2,4},{3,5},{4,6},{5,7},{6,8},{7,9},{8,10},{9,11},{10,12},{1... | collective-permute-start | bytes 786440 | tf_op jit(solution)/shard_map/ppermute | solution.py:170
  32.4 21.7 %collective-permute-start.2 = (bf16[256,512]{1,0:T(8,128)(2,1)S(1)}, bf16[256,512]{1,0:T(8,128)(2,1)S(1)}, u32[]{:S(2)}, u32[]{:S(2)}) collective-permute-start(bf16[256,512]{1,0:T(8,128)(2,1)S(1)} %get-tuple-element.22), channel_id=1, source_target_pairs={{1,3},{2,4},{3,5},{4,6},{5,7},{6,8},{7,9},{8,10},{9,11},{10,12},{1... | collective-permute-start | bytes 786440 | tf_op jit(solution)/shard_map/ppermute | solution.py:170
  54.0 10.6 %collective-permute-start.7 = (bf16[256,512]{1,0:T(8,128)(2,1)S(1)}, bf16[256,512]{1,0:T(8,128)(2,1)S(1)}, u32[]{:S(2)}, u32[]{:S(2)}) collective-permute-start(bf16[256,512]{1,0:T(8,128)(2,1)S(1)} %collective-permute-done.2.refs_6_), channel_id=1, source_target_pairs={{3,5},{4,6},{5,7},{6,8},{7,9},{8,10},{9,11},{10,12},{11,13},{12,14... | collective-permute-start | bytes 786440 | tf_op jit(solution)/shard_map/ppermute | solution.py:170
  54.1 13.4 %collective-permute-start.6 = (bf16[128,1024]{1,0:T(8,128)(2,1)S(1)}, bf16[128,1024]{1,0:T(8,128)(2,1)S(1)}, u32[]{:S(2)}, u32[]{:S(2)}) collective-permute-start(bf16[128,1024]{1,0:T(8,128)(2,1)S(1)} %slice.12), channel_id=1, source_target_pairs={{4,6},{5,7},{6,8},{7,9},{8,10},{9,11},{10,12},{11,13},{12,14},{13,... | collective-permute-start | bytes 786440 | tf_op jit(solution)/shard_map/ppermute | solution.py:170
  54.2 20.5 %collective-permute-start.5 = (bf16[256,512]{1,0:T(8,128)(2,1)S(1)}, bf16[256,512]{1,0:T(8,128)(2,1)S(1)}, u32[]{:S(2)}, u32[]{:S(2)}) collective-permute-start(bf16[256,512]{1,0:T(8,128)(2,1)S(1)} %collective-permute-done.3.refs_6_), channel_id=1, source_target_pairs={{3,5},{4,6},{5,7},{6,8},{7,9},{8,10},{9,11},{10,12},{11,13},{12,14... | collective-permute-start | bytes 786440 | tf_op jit(solution)/shard_map/ppermute | solution.py:170

commit v3 on v2

--- a/solution.py
+++ b/solution.py
@@ -88,8 +88,8 @@
         gather(head)
         if head == 0:
             fetch.wait()
-        for tile in range(2):
-            for member in range(GROUP):
+        for member in range(GROUP):
+            for tile in range(2):
                 rows = pl.ds(tile * TILE, TILE)
                 columns = pl.ds((head * GROUP + member) * HEAD_SIZE, HEAD_SIZE)
                 scores = lax.dot_general(

time: 82.2 us -> 82.2 us (level)
  no operation moved by 1% of the time
where the time goes in v3:
time: 82.2 us; the launch traced here: 82 us
  waiting for transfers between devices  55.4 us (67%)
  Pallas kernels  15.6 us (19%)
  starting transfers between devices  10.6 us (13%)
    ppermute x8, waiting for transfers between devices, ahead(): return lax.ppermute(value, AXES, pairs)  55.4 us
    pallas_call x2, Pallas kernels, attend(): pl.pallas_call(lambda *refs: attend_kernel(first_head, heads, *refs), gri...  14.4 us
    ppermute x8, starting transfers between devices, ahead(): return lax.ppermute(value, AXES, pairs)  10.6 us
  transfers between devices with their start and end apart: 8, of which 6 were waited for; matrix products, arithmetic and copies ran while one was open for 0% of the time, Pallas kernels for 9%

profile of v3, /device:TPU:16, one launch (start us, length us, event | category | flops | bytes accessed | tf_op | source)
XLA Modules:
  0.0 82.0 jit_solution(827207929515216680)
XLA Ops:
  0.0 0.0 copy-start
  0.0 1.2 %pack.1.refs_3_ = bf16[256,1024]{1,0:T(8,128)(2,1)S(1)} custom-call(bf16[256,512]{1,0:T(8,128)(2,1)} %keys.1, bf16[256,512]{1,0:T(8,128)(2,1)} %values.1), custom_call_target="tpu_custom_call" | custom-call | tf_op jit(solution)/shard_map/pack/pallas_call | solution.py:36
  1.2 0.1 collective-permute-start.1
  1.3 7.3 %collective-permute-start = (bf16[256,1024]{1,0:T(8,128)(2,1)S(1)}, bf16[256,1024]{1,0:T(8,128)(2,1)S(1)}, u32[]{:S(2)}, u32[]{:S(2)}) collective-permute-start(bf16[256,1024]{1,0:T(8,128)(2,1)S(1)} %pack.1.refs_3_), channel_id=1, source_target_pairs={{0,1},{1,2},{2,3},{3,4},{4,5},{5,6},{6,7},{7,8},{8,9},{9,10},{10,1... | collective-permute-start | bytes 1572872 | tf_op jit(solution)/shard_map/ppermute | solution.py:170
  8.6 0.0 copy-done
  8.6 0.1 dynamic-slice_bitcast_fusion
  8.7 11.2 %collective-permute-done.1.refs_5_ = bf16[256,1024]{1,0:T(8,128)(2,1)S(1)} collective-permute-done((bf16[256,1024]{1,0:T(8,128)(2,1)S(1)}, bf16[256,1024]{1,0:T(8,128)(2,1)S(1)}, u32[]{:S(2)}, u32[]{:S(2)}) %collective-permute-start.1) | collective-permute-done | bytes 524320 | tf_op jit(solution)/shard_map/ppermute | solution.py:170
  19.9 0.0 collective-permute-start.4
  19.9 0.1 compare_select_fusion.refs_1_
  20.0 9.5 %collective-permute-done.refs_4_ = bf16[256,1024]{1,0:T(8,128)(2,1)S(1)} collective-permute-done((bf16[256,1024]{1,0:T(8,128)(2,1)S(1)}, bf16[256,1024]{1,0:T(8,128)(2,1)S(1)}, u32[]{:S(2)}, u32[]{:S(2)}) %collective-permute-start) | collective-permute-done | bytes 524320 | tf_op jit(solution)/shard_map/ppermute | solution.py:170
  29.6 2.8 %collective-permute-start.3 = (bf16[256,512]{1,0:T(8,128)(2,1)S(1)}, bf16[256,512]{1,0:T(8,128)(2,1)S(1)}, u32[]{:S(2)}, u32[]{:S(2)}) collective-permute-start(bf16[256,512]{1,0:T(8,128)(2,1)S(1)} %get-tuple-element.21), channel_id=1, source_target_pairs={{1,3},{2,4},{3,5},{4,6},{5,7},{6,8},{7,9},{8,10},{9,11},{10,12},{1... | collective-permute-start | bytes 786440 | tf_op jit(solution)/shard_map/ppermute | solution.py:170
  32.4 0.1 collective-permute-start.2
  32.4 18.8 %collective-permute-done.3.refs_6_ = bf16[256,512]{1,0:T(8,128)(2,1)S(1)} collective-permute-done((bf16[256,512]{1,0:T(8,128)(2,1)S(1)}, bf16[256,512]{1,0:T(8,128)(2,1)S(1)}, u32[]{:S(2)}, u32[]{:S(2)}) %collective-permute-start.3) | collective-permute-done | bytes 262176 | tf_op jit(solution)/shard_map/ppermute | solution.py:170
  51.2 2.8 %collective-permute-done.2.refs_6_ = bf16[256,512]{1,0:T(8,128)(2,1)S(1)} collective-permute-done((bf16[256,512]{1,0:T(8,128)(2,1)S(1)}, bf16[256,512]{1,0:T(8,128)(2,1)S(1)}, u32[]{:S(2)}, u32[]{:S(2)}) %collective-permute-start.2) | collective-permute-done | bytes 262176 | tf_op jit(solution)/shard_map/ppermute | solution.py:170
  54.0 0.0 collective-permute-start.7
  54.0 0.0 collective-permute-done.4.refs_7_
  54.1 0.1 collective-permute-start.6
  54.2 0.3 collective-permute-start.5
  54.4 10.2 %collective-permute-done.7.refs_8_ = bf16[256,512]{1,0:T(8,128)(2,1)S(1)} collective-permute-done((bf16[256,512]{1,0:T(8,128)(2,1)S(1)}, bf16[256,512]{1,0:T(8,128)(2,1)S(1)}, u32[]{:S(2)}, u32[]{:S(2)}) %collective-permute-start.7) | collective-permute-done | bytes 262176 | tf_op jit(solution)/shard_map/ppermute | solution.py:170
  64.6 2.8 %collective-permute-done.6.refs_9_ = bf16[128,1024]{1,0:T(8,128)(2,1)S(1)} collective-permute-done((bf16[128,1024]{1,0:T(8,128)(2,1)S(1)}, bf16[128,1024]{1,0:T(8,128)(2,1)S(1)}, u32[]{:S(2)}, u32[]{:S(2)}) %collective-permute-start.6) | collective-permute-done | bytes 262176 | tf_op jit(solution)/shard_map/ppermute | solution.py:170
  67.4 7.2 %attend.2.refs_10_ = bf16[256,3584]{1,0:T(8,128)(2,1)} custom-call(s32[4,8]{1,0:T(4,128)} %refs_0_.3, f32[2,128,128]{2,1,0:T(8,128)S(1)} %compare_select_fusion.refs_1_, bf16[256,3584]{1,0:T(8,128)(2,1)} %refs_2_.3, bf16[256,1024]{1,0:T(8,128)(2,1)S(1)} %pack.1.refs_3_, bf16[256,1024]{1,0:T(8,128)(2,1)S(1)} %collective-permute-done.refs_4_, ...), custom_call_target="tpu_custom_call" | custom-call | flops 1048576 | bytes 65536 | tf_op jit(solution)/shard_map/attend/pallas_call | solution.py:137
  74.6 0.0 collective-permute-done.5.refs_8_
  74.7 7.2 %attend.3 = bf16[256,3584]{1,0:T(8,128)(2,1)} custom-call(s32[4,8]{1,0:T(4,128)} %refs_0_.3, f32[2,128,128]{2,1,0:T(8,128)S(1)} %compare_select_fusion.refs_1_, bf16[256,3584]{1,0:T(8,128)(2,1)} %refs_2_.3, bf16[256,1024]{1,0:T(8,128)(2,1)S(1)} %pack.1.refs_3_, bf16[256,1024]{1,0:T(8,128)(2,1)S(1)} %collective-permute-done.refs_4_, ...), custom_call_target="tpu_custom_call", output_to_operand_aliasing={{}: (10, {})} | custom-call | flops 1048576 | bytes 65536 | tf_op jit(solution)/shard_map/attend/pallas_call | solution.py:137
  (2 shorter events, 0.1 us)
Async XLA Ops:
  0.0 8.6 %copy-start = (s32[65536]{0:T(1024)S(1)}, s32[65536]{0:T(1024)}, u32[]{:S(2)}) copy-start(s32[65536]{0:T(1024)} %param.9) | copy-start | bytes 786436
  1.2 18.7 %collective-permute-start.1 = (bf16[256,1024]{1,0:T(8,128)(2,1)S(1)}, bf16[256,1024]{1,0:T(8,128)(2,1)S(1)}, u32[]{:S(2)}, u32[]{:S(2)}) collective-permute-start(bf16[256,1024]{1,0:T(8,128)(2,1)S(1)} %pack.1.refs_3_), channel_id=1, source_target_pairs={{0,2},{1,3},{2,4},{3,5},{4,6},{5,7},{6,8},{7,9},{8,10},{9,11},{10,... | collective-permute-start | bytes 1572872 | tf_op jit(solution)/shard_map/ppermute | solution.py:170
  1.3 28.2 %collective-permute-start = (bf16[256,1024]{1,0:T(8,128)(2,1)S(1)}, bf16[256,1024]{1,0:T(8,128)(2,1)S(1)}, u32[]{:S(2)}, u32[]{:S(2)}) collective-permute-start(bf16[256,1024]{1,0:T(8,128)(2,1)S(1)} %pack.1.refs_3_), channel_id=1, source_target_pairs={{0,1},{1,2},{2,3},{3,4},{4,5},{5,6},{6,7},{7,8},{8,9},{9,10},{10,1... | collective-permute-start | bytes 1572872 | tf_op jit(solution)/shard_map/ppermute | solution.py:170
  19.9 34.1 %collective-permute-start.4 = (bf16[256,1024]{1,0:T(8,128)(2,1)S(1)}, bf16[256,1024]{1,0:T(8,128)(2,1)S(1)}, u32[]{:S(2)}, u32[]{:S(2)}) collective-permute-start(bf16[256,1024]{1,0:T(8,128)(2,1)S(1)} %collective-permute-done.1.refs_5_), channel_id=1, source_target_pairs={{2,4},{3,5},{4,6},{5,7},{6,8},{7,9},{8,10},{9,11},{10,12},{11,13},... | collective-permute-start | bytes 1572872 | tf_op jit(solution)/shard_map/ppermute | solution.py:170
  29.6 21.6 %collective-permute-start.3 = (bf16[256,512]{1,0:T(8,128)(2,1)S(1)}, bf16[256,512]{1,0:T(8,128)(2,1)S(1)}, u32[]{:S(2)}, u32[]{:S(2)}) collective-permute-start(bf16[256,512]{1,0:T(8,128)(2,1)S(1)} %get-tuple-element.21), channel_id=1, source_target_pairs={{1,3},{2,4},{3,5},{4,6},{5,7},{6,8},{7,9},{8,10},{9,11},{10,12},{1... | collective-permute-start | bytes 786440 | tf_op jit(solution)/shard_map/ppermute | solution.py:170
  32.4 21.7 %collective-permute-start.2 = (bf16[256,512]{1,0:T(8,128)(2,1)S(1)}, bf16[256,512]{1,0:T(8,128)(2,1)S(1)}, u32[]{:S(2)}, u32[]{:S(2)}) collective-permute-start(bf16[256,512]{1,0:T(8,128)(2,1)S(1)} %get-tuple-element.22), channel_id=1, source_target_pairs={{1,3},{2,4},{3,5},{4,6},{5,7},{6,8},{7,9},{8,10},{9,11},{10,12},{1... | collective-permute-start | bytes 786440 | tf_op jit(solution)/shard_map/ppermute | solution.py:170
  54.0 10.6 %collective-permute-start.7 = (bf16[256,512]{1,0:T(8,128)(2,1)S(1)}, bf16[256,512]{1,0:T(8,128)(2,1)S(1)}, u32[]{:S(2)}, u32[]{:S(2)}) collective-permute-start(bf16[256,512]{1,0:T(8,128)(2,1)S(1)} %collective-permute-done.2.refs_6_), channel_id=1, source_target_pairs={{3,5},{4,6},{5,7},{6,8},{7,9},{8,10},{9,11},{10,12},{11,13},{12,14... | collective-permute-start | bytes 786440 | tf_op jit(solution)/shard_map/ppermute | solution.py:170
  54.1 13.4 %collective-permute-start.6 = (bf16[128,1024]{1,0:T(8,128)(2,1)S(1)}, bf16[128,1024]{1,0:T(8,128)(2,1)S(1)}, u32[]{:S(2)}, u32[]{:S(2)}) collective-permute-start(bf16[128,1024]{1,0:T(8,128)(2,1)S(1)} %slice.12), channel_id=1, source_target_pairs={{4,6},{5,7},{6,8},{7,9},{8,10},{9,11},{10,12},{11,13},{12,14},{13,... | collective-permute-start | bytes 786440 | tf_op jit(solution)/shard_map/ppermute | solution.py:170
  54.2 20.5 %collective-permute-start.5 = (bf16[256,512]{1,0:T(8,128)(2,1)S(1)}, bf16[256,512]{1,0:T(8,128)(2,1)S(1)}, u32[]{:S(2)}, u32[]{:S(2)}) collective-permute-start(bf16[256,512]{1,0:T(8,128)(2,1)S(1)} %collective-permute-done.3.refs_6_), channel_id=1, source_target_pairs={{3,5},{4,6},{5,7},{6,8},{7,9},{8,10},{9,11},{10,12},{11,13},{12,14... | collective-permute-start | bytes 786440 | tf_op jit(solution)/shard_map/ppermute | solution.py:170
